TPU v7x, 256 devices: a whole 4x4x8 slice. The times are simulated.
256 devices in a mesh: slide: 16 (over x, y_hi, core), rep: 16 (over z, y_lo).
Axes of the slice: x: 4, y: 4 (y_hi: 2, y_lo: 2; y = y_hi * 2 + y_lo), z: 8, core: 2. Of those that a mesh axis runs over, the one named last changes fastest.
Arguments:
- tile_images: bfloat16 [1024, 32, 32, 384], P(('slide', 'rep')), may hold values from -6 to 6
- cotangent: bfloat16 [1024, 32, 32, 384], P(('slide', 'rep')), may hold values from -0.1875 to 0.1875
- depth_kernel: bfloat16 [7, 7, 384], replicated, may hold values from -0.875 to 0.875
- depth_bias: float32 [384], replicated, may hold values from -3 to 3
- norm_gain: float32 [384], replicated, may hold values from 0.5 to 2
- norm_bias: float32 [384], replicated, may hold values from -3 to 3
- expand_weight: bfloat16 [1536, 384], replicated, may hold values from -0.3125 to 0.3125
- expand_bias: float32 [1536], replicated, may hold values from -3 to 3
- project_weight: bfloat16 [1536, 384], replicated, may hold values from -0.15625 to 0.15625
- layer_scale: float32 [384], replicated, may hold values from 0.1 to 1
- tile_counts: int32 [16, 16], P('slide', 'rep'), may hold values from 1 to 4, as said below
- send_list: int32 [16, 16, 16], P('slide', 'rep'), may hold values from -1 to 31, as said below
Outputs:
- grad_expand: float32 [1536, 384], P(('slide', 'rep'))
- grad_project: float32 [1536, 384], P(('slide', 'rep'))
Inputs may be any that keep to these rules, and one draw needn't show every extreme that they name: Every device holds its tiles in its first tile_counts slots; some device holds 4 tiles and some device one. `send_list`: the blocks that a device names are distinct and lie in its first tile_counts tiles; each device names at least one block and at most 16, at most one for each destination, and some device names 16; each device (d, r) is named as destination by at most 5 devices, and some device by exactly 5.
All inputs are finite; a program needn't handle non-finite values.
Results may differ from a plain program's by a relative error of at most 0.0055.
Values may be sent and summed in bfloat16 or wider, within the bound.
No kernel may reach another device: no remote copies, remote signals or barrier semaphores. Data moves between devices by JAX's collectives and lax.ppermute only.
A program may use at most 128 MiB of HBM per device.

v0:
```python
import jax
import jax.numpy as jnp
from jax import lax
from jax.experimental import pallas as pl
from jax.experimental.pallas import tpu as pltpu
from jax.sharding import PartitionSpec as P

BANDS = 8
MARGIN = 3
BAND_ROWS = 4
BAND_TOK = 128
SLOTS = 16
GROUP = 2
KEPT = 9
FIRST = 2
ROWS = BAND_ROWS + 2 * MARGIN
HID_STEP = 768
SPAN = GROUP * BAND_TOK
GROUPS = SLOTS // GROUP
PAIRS = 8
CHUNK = 96
PLANE = 16
SHARE = 6
DEAL = 16

root_half = 0.7071067811865476
inv_root_tau = 0.3989422804014327

INNER = (((1,), (1,)), ((), ()))
PLAIN = (((1,), (0,)), ((), ()))


def half_copies(weight_hbm, weight, core, sems):
    copies = []
    for half in range(2):
        for pair in range(PAIRS):
            first = pl.multiple_of((2 * pair + (core ^ half)) * CHUNK, CHUNK)
            copies.append(
                pltpu.make_async_copy(
                    weight_hbm.at[pl.ds(first, CHUNK)],
                    weight.at[pl.ds((half * PAIRS + pair) * CHUNK, CHUNK)],
                    sems.at[half, pair],
                )
            )
    return copies


def pack_list(slots_ref, order_ref):
    listed = jnp.int32(0)
    for slot in range(SLOTS):
        block = slots_ref[slot]
        order_ref[listed] = jnp.maximum(block, 0)
        listed = listed + jnp.where(block >= 0, 1, 0)
    return listed


def block_copies(order_ref, index, images_hbm, cotan_hbm, images, cotans, sems):
    block = order_ref[index]
    tile = block // BANDS
    band = block % BANDS
    first = band * BAND_ROWS
    above = pltpu.make_async_copy(
        images_hbm.at[tile, pl.ds(first - MARGIN, MARGIN)], images.at[pl.ds(0, MARGIN)], sems.at[0]
    )
    middle = pltpu.make_async_copy(
        images_hbm.at[tile, pl.ds(first, BAND_ROWS)], images.at[pl.ds(MARGIN, BAND_ROWS)], sems.at[1]
    )
    below = pltpu.make_async_copy(
        images_hbm.at[tile, pl.ds(first + BAND_ROWS, MARGIN)],
        images.at[pl.ds(MARGIN + BAND_ROWS, MARGIN)],
        sems.at[2],
    )
    error = pltpu.make_async_copy(cotan_hbm.at[tile, pl.ds(first, BAND_ROWS)], cotans, sems.at[3])
    return band, above, middle, below, error


def start_block(band, above, middle, below, error):
    pl.when(band > 0)(above.start)
    middle.start()
    pl.when(band < BANDS - 1)(below.start)
    error.start()


def conv_norm(image, band, taps, conv_out, depth_bias, gain, norm_bias):
    _, side, channels = image.shape

    @pl.when(band == 0)
    def _():
        image[:MARGIN] = jnp.zeros((MARGIN, side, channels), image.dtype)

    @pl.when(band == BANDS - 1)
    def _():
        image[MARGIN + BAND_ROWS : ROWS] = jnp.zeros((MARGIN, side, channels), image.dtype)

    column = lax.broadcasted_iota(jnp.int32, (8, 128), 0)
    for lanes in range(0, channels, 128):
        part = slice(lanes, lanes + 128)
        for row in range(BAND_ROWS):
            sums = [None] * 7
            for dy in range(7):
                x = image[row + dy, :, part].astype(jnp.float32)
                for dx in range(7):
                    term = x * taps[dy, dx : dx + 1, part]
                    sums[dx] = term if sums[dx] is None else sums[dx] + term
            total = sums[MARGIN] + depth_bias[:, part]
            for dx in range(-MARGIN, MARGIN + 1):
                if dx != 0:
                    moved = pltpu.roll(sums[dx + MARGIN], (-dx) % side, 0)
                    if dx < 0:
                        edge = jnp.where(column + dx >= 0, moved[:8], 0.0)
                        moved = jnp.concatenate([edge, moved[8:]], axis=0)
                    else:
                        edge = jnp.where(column + dx < 8, moved[side - 8 :], 0.0)
                        moved = jnp.concatenate([moved[: side - 8], edge], axis=0)
                    total = total + moved
            conv_out[row * side : (row + 1) * side, part] = total
    mixed = conv_out[...]
    centre = jnp.mean(mixed, axis=-1, keepdims=True)
    away = mixed - centre
    spread = jnp.mean(away * away, axis=-1, keepdims=True)
    return (away * lax.rsqrt(spread + 1e-06) * gain + norm_bias).astype(jnp.bfloat16)


def scale_errors(errors, scale):
    rows, side, channels = errors.shape
    flat = errors[...].reshape(rows * side, channels)
    return (flat.astype(jnp.float32) * scale).astype(jnp.bfloat16)


def conv_blocks(low, high, refs, between):
    (
        count_ref,
        images_hbm,
        cotan_hbm,
        taps_ref,
        depth_bias_ref,
        gain_ref,
        norm_bias_ref,
        scale_ref,
        acts_hbm,
        images,
        cotans,
        taps,
        acts,
        conv_out,
        order_ref,
        image_sems,
        acts_sems,
    ) = refs
    channels = images_hbm.shape[3]

    def copies(index):
        return block_copies(
            order_ref,
            index,
            images_hbm,
            cotan_hbm,
            images.at[index - low],
            cotans.at[index - low],
            image_sems.at[index - low],
        )

    @pl.loop(low, high)
    def _(index):
        start_block(*copies(index))

    taps[...] = taps_ref[...].astype(jnp.float32)
    depth_bias = depth_bias_ref[...].reshape(1, channels)
    gain = gain_ref[...].reshape(1, channels)
    norm_bias = norm_bias_ref[...].reshape(1, channels)
    scale = scale_ref[...].reshape(1, channels) / count_ref[0].astype(jnp.float32)

    def acts_copy(index):
        rows = pl.ds(pl.multiple_of((index - low) * BAND_TOK, BAND_TOK), BAND_TOK)
        return pltpu.make_async_copy(
            acts.at[:, rows], acts_hbm.at[:, rows], acts_sems.at[index - low]
        )

    @pl.loop(low, high)
    def _(index):
        band, above, middle, below, error = copies(index)
        pl.when(band > 0)(above.wait)
        middle.wait()
        pl.when(band < BANDS - 1)(below.wait)
        rows = pl.ds(pl.multiple_of((index - low) * BAND_TOK, BAND_TOK), BAND_TOK)
        acts[0, rows, :] = conv_norm(
            images.at[index - low], band, taps, conv_out, depth_bias, gain, norm_bias
        )
        error.wait()
        acts[1, rows, :] = scale_errors(cotans.at[index - low], scale)
        acts_copy(index).start()
        if between is not None:
            pl.when(index == low)(between)

    @pl.loop(low, high)
    def _(index):
        acts_copy(index).wait()


def first_kernel(slots_ref, *refs):
    (packed_hbm, acts_hbm), packed, (sems, out_sems) = refs[8:10], refs[15], refs[19:]
    refs = refs[:8] + (acts_hbm,) + refs[10:15] + refs[16:19]
    images_hbm, cotan_hbm, order_ref = refs[1], refs[2], refs[14]
    listed = pack_list(slots_ref, order_ref)

    def copies(index):
        place = packed.at[index - KEPT]
        return block_copies(
            order_ref,
            index,
            images_hbm,
            cotan_hbm,
            place.at[pl.ds(0, ROWS)],
            place.at[pl.ds(ROWS, BAND_ROWS)],
            sems.at[index - KEPT],
        )

    def out_copy(index):
        place = index - KEPT
        return pltpu.make_async_copy(packed.at[place], packed_hbm.at[place], out_sems.at[place])

    @pl.loop(KEPT, listed)
    def _(index):
        start_block(*copies(index))

    def send_out():
        @pl.loop(KEPT, listed)
        def _(index):
            band, above, middle, below, error = copies(index)
            pl.when(band > 0)(above.wait)
            middle.wait()
            pl.when(band < BANDS - 1)(below.wait)
            error.wait()
            out_copy(index).start()

    conv_blocks(0, jnp.minimum(listed, FIRST), refs, send_out)

    @pl.loop(KEPT, listed)
    def _(index):
        out_copy(index).wait()


def other_kernel(slots_ref, *refs):
    listed = pack_list(slots_ref, refs[14])
    conv_blocks(FIRST, jnp.maximum(jnp.minimum(listed, KEPT), FIRST), refs, None)


def train_kernel(
    slots_ref,
    there_ref,
    count_there_ref,
    core_ref,
    first_hbm,
    other_hbm,
    packed_hbm,
    taps_ref,
    depth_bias_ref,
    gain_ref,
    norm_bias_ref,
    scale_ref,
    expand_hbm,
    expand_bias_ref,
    project_hbm,
    keep_hbm,
    send_hbm,
    packed,
    taps,
    acts,
    conv_out,
    expand,
    project,
    grad,
    bias_all,
    bias_ref,
    out,
    order_ref,
    packed_sems,
    acts_sems,
    weight_sems,
    out_sems,
):
    channels = packed_hbm.shape[3]
    core = core_ref[0]
    listed_there = pack_list(there_ref, order_ref)
    listed = jnp.int32(0)
    for slot in range(SLOTS):
        listed = listed + jnp.where(slots_ref[slot] >= 0, 1, 0)
    own = jnp.minimum(listed, KEPT)
    taken = jnp.maximum(listed_there - KEPT, 0)

    def packed_copy(place):
        return pltpu.make_async_copy(packed_hbm.at[place], packed.at[place], packed_sems.at[place])

    def acts_copy(source, low, index):
        rows = pl.ds(pl.multiple_of((index - low) * BAND_TOK, BAND_TOK), BAND_TOK)
        there = pl.ds(pl.multiple_of(index * BAND_TOK, BAND_TOK), BAND_TOK)
        return pltpu.make_async_copy(source.at[:, rows], acts.at[:, there], acts_sems.at[index])

    @pl.loop(0, taken)
    def _(index):
        packed_copy(index).start()

    weight_copies = half_copies(expand_hbm, expand, core, weight_sems.at[0])
    weight_copies += half_copies(project_hbm, project, core, weight_sems.at[1])
    for copy in weight_copies:
        copy.start()

    early = jnp.minimum(own, FIRST)

    @pl.loop(0, early)
    def _(index):
        acts_copy(first_hbm, 0, index).start()

    @pl.loop(FIRST, own)
    def _(index):
        acts_copy(other_hbm, FIRST, index).start()

    hidden = expand_bias_ref.shape[0]
    for first in range(0, hidden, 128):
        row = expand_bias_ref[pl.ds(first, 128)].reshape(1, 128)
        bias_all[pl.ds(first, 128), :] = jnp.broadcast_to(row, (128, 128)).T
    for half in range(2):
        for pair in range(PAIRS):
            rows = pl.ds(pl.multiple_of((2 * pair + (core ^ half)) * CHUNK, CHUNK), CHUNK)
            bias_ref[pl.ds((half * PAIRS + pair) * CHUNK, CHUNK), :] = bias_all[rows, :]
    taps[...] = taps_ref[...].astype(jnp.float32)
    depth_bias = depth_bias_ref[...].reshape(1, channels)
    gain = gain_ref[...].reshape(1, channels)
    norm_bias = norm_bias_ref[...].reshape(1, channels)
    scale = scale_ref[...].reshape(1, channels) / count_there_ref[0].astype(jnp.float32)
    grad[...] = jnp.zeros(grad.shape, jnp.float32)

    @pl.loop(0, taken)
    def _(index):
        packed_copy(index).wait()
        rows = pl.ds(pl.multiple_of((own + index) * BAND_TOK, BAND_TOK), BAND_TOK)
        band = order_ref[KEPT + index] % BANDS
        acts[0, rows, :] = conv_norm(
            packed.at[index, pl.ds(0, ROWS)], band, taps, conv_out, depth_bias, gain, norm_bias
        )
        acts[1, rows, :] = scale_errors(packed.at[index, pl.ds(ROWS, BAND_ROWS)], scale)

    total = own + taken

    @pl.when(total % GROUP != 0)
    def _():
        rows = pl.ds(pl.multiple_of(total * BAND_TOK, BAND_TOK), BAND_TOK)
        acts[:, rows, :] = jnp.zeros((2, BAND_TOK, channels), acts.dtype)

    for copy in weight_copies:
        copy.wait()

    @pl.loop(0, early)
    def _(index):
        acts_copy(first_hbm, 0, index).wait()

    @pl.loop(FIRST, own)
    def _(index):
        acts_copy(other_hbm, FIRST, index).wait()

    half = hidden // 2

    @pl.loop(0, (total + GROUP - 1) // GROUP)
    def _(group):
        rows = pl.ds(pl.multiple_of(group * SPAN, SPAN), SPAN)
        flat_in = acts[0, rows, :]
        flat_err = acts[1, rows, :]
        for start in range(0, 2 * half, HID_STEP):
            units = slice(start, start + HID_STEP)
            pre_act = lax.dot_general(
                expand[units, :], flat_in, INNER, preferred_element_type=jnp.float32
            )
            back_grad = lax.dot_general(
                project[units, :], flat_err, INNER, preferred_element_type=jnp.float32
            )
            pre_act = pre_act + jnp.concatenate([bias_ref[units, :]] * (SPAN // 128), axis=1)
            share = 0.5 * (1.0 + lax.erf(pre_act * root_half))
            activated = (pre_act * share).astype(jnp.bfloat16)
            bell = jnp.exp(-0.5 * pre_act * pre_act) * inv_root_tau
            slope_term = (back_grad * (share + pre_act * bell)).astype(jnp.bfloat16)
            grad[0, units, :] += lax.dot_general(
                slope_term, flat_in, PLAIN, preferred_element_type=jnp.float32
            )
            grad[1, units, :] += lax.dot_general(
                activated, flat_err, PLAIN, preferred_element_type=jnp.float32
            )

    def out_copy(half, pair):
        return pltpu.make_async_copy(
            out.at[half, pair], (keep_hbm, send_hbm)[half].at[pair], out_sems.at[half, pair]
        )

    for half in (1, 0):
        for pair in range(PAIRS):
            rows = slice((half * PAIRS + pair) * CHUNK, (half * PAIRS + pair + 1) * CHUNK)
            out[half, pair] = grad[:, rows, :].astype(out.dtype)
            out_copy(half, pair).start()
    for half in (1, 0):
        for pair in range(PAIRS):
            out_copy(half, pair).wait()


SMEM = pl.BlockSpec(memory_space=pltpu.SMEM)
VMEM = pl.BlockSpec(memory_space=pltpu.VMEM)
HBM = pl.BlockSpec(memory_space=pl.ANY)


def params(mib):
    return pltpu.CompilerParams(vmem_limit_bytes=mib * 2**20)


def conv_scratch(blocks, side, channels):
    bf16, f32 = jnp.bfloat16, jnp.float32
    return [
        pltpu.VMEM((blocks, ROWS, side, channels), bf16),
        pltpu.VMEM((blocks, BAND_ROWS, side, channels), bf16),
        pltpu.VMEM((7, 7, channels), f32),
        pltpu.VMEM((2, blocks * BAND_TOK, channels), bf16),
        pltpu.VMEM((BAND_TOK, channels), f32),
    ]


def conv_first(slots, count, tile_images, cotangent, conv_weights, scale):
    side, channels = tile_images.shape[1], tile_images.shape[3]
    packed = (SLOTS - KEPT, ROWS + BAND_ROWS, side, channels)
    return pl.pallas_call(
        first_kernel,
        out_shape=(
            jax.ShapeDtypeStruct(packed, jnp.bfloat16),
            jax.ShapeDtypeStruct((2, FIRST * BAND_TOK, channels), jnp.bfloat16),
        ),
        in_specs=[SMEM] * 2 + [HBM] * 2 + [VMEM] * 5,
        out_specs=[HBM] * 2,
        scratch_shapes=conv_scratch(FIRST, side, channels)
        + [
            pltpu.VMEM(packed, jnp.bfloat16),
            pltpu.SMEM((SLOTS + 1,), jnp.int32),
            pltpu.SemaphoreType.DMA((FIRST, 4)),
            pltpu.SemaphoreType.DMA((FIRST,)),
            pltpu.SemaphoreType.DMA((SLOTS - KEPT, 4)),
            pltpu.SemaphoreType.DMA((SLOTS - KEPT,)),
        ],
        compiler_params=params(56),
        name="conv_first",
    )(slots, count, tile_images, cotangent, *conv_weights, scale)


def conv_other(slots, count, tile_images, cotangent, conv_weights, scale):
    side, channels = tile_images.shape[1], tile_images.shape[3]
    blocks = KEPT - FIRST
    return pl.pallas_call(
        other_kernel,
        out_shape=jax.ShapeDtypeStruct((2, blocks * BAND_TOK, channels), jnp.bfloat16),
        in_specs=[SMEM] * 2 + [HBM] * 2 + [VMEM] * 5,
        out_specs=HBM,
        scratch_shapes=conv_scratch(blocks, side, channels)
        + [
            pltpu.SMEM((SLOTS + 1,), jnp.int32),
            pltpu.SemaphoreType.DMA((blocks, 4)),
            pltpu.SemaphoreType.DMA((blocks,)),
        ],
        compiler_params=params(56),
        cost_estimate=pl.CostEstimate(flops=8 * 10**9, bytes_accessed=10**7, transcendentals=0),
        name="conv_other",
    )(slots, count, tile_images, cotangent, *conv_weights, scale)


def train(
    slots, there, count_there, core, acts, packed, conv_weights, scale, expand_weight, expand_bias,
    project_weight,
):
    hidden, channels = expand_weight.shape
    bf16, f32 = jnp.bfloat16, jnp.float32
    return pl.pallas_call(
        train_kernel,
        out_shape=[jax.ShapeDtypeStruct((PAIRS, 2, CHUNK, channels), bf16)] * 2,
        in_specs=[SMEM] * 4 + [HBM] * 3 + [VMEM] * 5 + [HBM, VMEM, HBM],
        out_specs=[HBM, HBM],
        scratch_shapes=[
            pltpu.VMEM(packed.shape, bf16),
            pltpu.VMEM((7, 7, channels), f32),
            pltpu.VMEM((2, SLOTS * BAND_TOK, channels), bf16),
            pltpu.VMEM((BAND_TOK, channels), f32),
            pltpu.VMEM((hidden, channels), bf16),
            pltpu.VMEM((hidden, channels), bf16),
            pltpu.VMEM((2, hidden, channels), f32),
            pltpu.VMEM((hidden, 128), f32),
            pltpu.VMEM((hidden, 128), f32),
            pltpu.VMEM((2, PAIRS, 2, CHUNK, channels), bf16),
            pltpu.SMEM((SLOTS + 1,), jnp.int32),
            pltpu.SemaphoreType.DMA((SLOTS - KEPT,)),
            pltpu.SemaphoreType.DMA((SLOTS,)),
            pltpu.SemaphoreType.DMA((2, 2, PAIRS)),
            pltpu.SemaphoreType.DMA((2, PAIRS)),
        ],
        compiler_params=params(56),
        cost_estimate=pl.CostEstimate(flops=9 * 10**9, bytes_accessed=10**7, transcendentals=0),
        name="train",
    )(
        slots, there, count_there, core, *acts, packed, *conv_weights, scale, expand_weight,
        expand_bias, project_weight,
    )


def deal_kernel(got_ref, out):
    total = got_ref[0].astype(jnp.float32)
    for source in range(1, PAIRS):
        total = total + got_ref[source].astype(jnp.float32)
    total = total.astype(jnp.bfloat16)
    row = lax.broadcasted_iota(jnp.int32, (PLANE * DEAL, CHUNK), 0)
    source = lax.broadcasted_iota(jnp.int32, (PLANE * DEAL, CHUNK), 1)
    place = row & (DEAL - 1)
    first = (row >> 4) * SHARE
    dealt = None
    for which in range(2):
        here = place - which * SHARE
        pick = (source == first + here) & (here >= 0) & (here < SHARE)
        part = lax.dot_general(
            jnp.where(pick, 1.0, 0.0).astype(jnp.bfloat16),
            total[which],
            PLAIN,
            preferred_element_type=jnp.float32,
        )
        dealt = part if dealt is None else dealt + part
    out[...] = dealt.astype(jnp.bfloat16).reshape(out.shape)


def deal(got):
    channels = got.shape[-1]
    return pl.pallas_call(
        deal_kernel,
        out_shape=jax.ShapeDtypeStruct((PLANE, DEAL, channels), jnp.bfloat16),
        in_specs=[VMEM],
        out_specs=VMEM,
        compiler_params=params(8),
        name="deal",
    )(got)


def last_kernel(got_ref, in_ref, out_ref):
    total = got_ref[0].astype(jnp.float32)
    for source in range(1, PLANE):
        total = total + got_ref[source].astype(jnp.float32)
    in_ref[...] = total[:SHARE]
    out_ref[...] = total[SHARE : 2 * SHARE]


def last(got):
    share = jax.ShapeDtypeStruct((SHARE, got.shape[-1]), jnp.float32)
    return pl.pallas_call(
        last_kernel,
        out_shape=[share, share],
        in_specs=[VMEM],
        out_specs=[VMEM, VMEM],
        compiler_params=params(4),
        name="last",
    )(got)


def over_chips(a):
    cores = [[place + core for place in range(0, SLOTS, 2)] for core in range(2)]
    return lax.all_to_all(a, "slide", 0, 0, tiled=True, axis_index_groups=cores)


def per_device(
    tile_images,
    cotangent,
    depth_kernel,
    depth_bias,
    norm_gain,
    norm_bias,
    expand_weight,
    expand_bias,
    project_weight,
    layer_scale,
    tile_counts,
    send_list,
):
    slide = lax.axis_index("slide").astype(jnp.int32)
    core = (slide & 1).reshape(1)
    slots = send_list.reshape(-1)
    count = tile_counts.reshape(-1)
    conv_weights = (depth_kernel, depth_bias, norm_gain, norm_bias)
    swap = [(i, i ^ 1) for i in range(16)]
    there = lax.ppermute(slots, "slide", swap)
    count_there = lax.ppermute(count, "slide", swap)
    packed, first = conv_first(
        slots, count, tile_images, cotangent, conv_weights, layer_scale
    )
    packed = lax.ppermute(packed, "slide", swap)
    other = conv_other(slots, count, tile_images, cotangent, conv_weights, layer_scale)
    keep, send = train(
        slots, there, count_there, core, (first, other), packed, conv_weights, layer_scale,
        expand_weight, expand_bias, project_weight,
    )
    got = lax.ppermute(send, "slide", swap)
    both = (keep.astype(jnp.float32) + got.astype(jnp.float32)).astype(jnp.bfloat16)
    got = deal(over_chips(both))
    return tuple(last(lax.all_to_all(got, "rep", 0, 0, tiled=True)))


def solution(mesh):
    in_specs = (
        P(("slide", "rep"), None, None, None),
        P(("slide", "rep"), None, None, None),
        P(),
        P(),
        P(),
        P(),
        P(),
        P(),
        P(),
        P(),
        P("slide", "rep"),
        P("slide", "rep", None),
    )
    out_specs = (P(("slide", "rep"), None), P(("slide", "rep"), None))
    return jax.shard_map(
        per_device, mesh=mesh, in_specs=in_specs, out_specs=out_specs, check_vma=False
    )
```

profile of v0, /device:TPU:2, one launch (start us, length us, event | category | flops | bytes accessed | tf_op | source)
XLA Modules:
  0.0 83.6 jit_solution(17499405503934591809)
XLA Ops:
  1.3 0.0 copy-start
  1.3 5.0 %conv_first.1 = (bf16[7,14,32,384]{3,2,1,0:T(8,128)(2,1)}, bf16[2,256,384]{2,1,0:T(8,128)(2,1)}) custom-call(s32[16]{0:T(128)} %bitcast.5, s32[1]{0:T(128)} %bitcast.3.refs_0_, bf16[4,32,32,384]{3,2,1,0:T(8,128)(2,1)} %refs_1_.3, bf16[4,32,32,384]{3,2,1,0:T(8,128)(2,1)} %refs_2_.3, bf16[7,7,384]{2,1,0:T(8,128)(2,1)} %taps_ref.1, f32[384]{0:T(512)} %depth_bias_ref.1, ...), custom_call_target="tpu_custom_call" | custom-call | tf_op jit(solution)/shard_map/conv_first/pallas_call | solution.py:426
  6.3 0.1 collective-permute-start.2
  6.4 0.0 copy-done
  6.4 0.5 collective-permute-start
  6.9 0.1 collective-permute-start.1
  7.0 4.9 %conv_other.1.other_hbm = bf16[2,896,384]{2,1,0:T(8,128)(2,1)} custom-call(s32[16]{0:T(128)} %bitcast.6, s32[1]{0:T(128)} %bitcast.4.refs_0_, bf16[4,32,32,384]{3,2,1,0:T(8,128)(2,1)} %refs_1_.3, bf16[4,32,32,384]{3,2,1,0:T(8,128)(2,1)} %refs_2_.3, bf16[7,7,384]{2,1,0:T(8,128)(2,1)} %taps_ref.1, f32[384]{0:T(512)} %depth_bias_ref.1, f32[384]{0:T(512)} %gain_ref.1, ...), custom_call_target="tpu_custom_call" | custom-call | flops 8000000000 | bytes 10000000 | tf_op jit(solution)/shard_map/conv_other/pallas_call | solution.py:451
  11.8 0.0 collective-permute-done.1.count_there_ref
  11.8 0.0 collective-permute-done.there_ref
  11.9 0.0 copy-start.2
  11.9 0.0 collective-permute-done.2.packed_hbm
  11.9 0.0 copy-start.1
  11.9 0.5 copy-done.2
  12.4 0.9 %copy-done.1 = bf16[7,14,32,384]{3,2,1,0:T(8,128)(2,1)} copy-done((bf16[7,14,32,384]{3,2,1,0:T(8,128)(2,1)}, bf16[7,14,32,384]{3,2,1,0:T(8,128)(2,1)S(1)}, u32[]{:S(2)}) %copy-start.1) | copy-done | bytes 2408472
  13.3 9.9 %train.1 = (bf16[8,2,96,384]{3,2,1,0:T(8,128)(2,1)}, bf16[8,2,96,384]{3,2,1,0:T(8,128)(2,1)}) custom-call(s32[16]{0:T(128)} %bitcast.7, s32[16]{0:T(128)} %copy-done.2, s32[1]{0:T(128)} %collective-permute-done.1.count_there_ref, s32[1]{0:T(128)} %bitcast.2.core_ref, bf16[2,256,384]{2,1,0:T(8,128)(2,1)} %get-tuple-element.6.first_hbm, ...), custom_call_target="tpu_custom_call" | custom-call | flops 8999999488 | bytes 10000000 | tf_op jit(solution)/shard_map/train/pallas_call | solution.py:474
  23.2 0.1 collective-permute-start.3
  23.3 3.0 %collective-permute-done.3 = bf16[8,2,96,384]{3,2,1,0:T(8,128)(2,1)S(1)} collective-permute-done((bf16[8,2,96,384]{3,2,1,0:T(8,128)(2,1)}, bf16[8,2,96,384]{3,2,1,0:T(8,128)(2,1)S(1)}, u32[]{:S(2)}, u32[]{:S(2)}) %collective-permute-start.3) | collective-permute-done | bytes 1179680 | tf_op jit(solution)/shard_map/ppermute | solution.py:596
  26.3 1.6 %add_convert_fusion = bf16[8,2,96,384]{3,2,1,0:T(8,128)(2,1)S(1)} fusion(bf16[8,2,96,384]{3,2,1,0:T(8,128)(2,1)S(1)} %collective-permute-done.3, bf16[8,2,96,384]{3,2,1,0:T(8,128)(2,1)} %get-tuple-element.8), kind=kLoop, calls=%fused_computation | loop fusion | flops 2359296 | bytes 3538944 | tf_op jit(solution)/shard_map/convert_element_type | solution.py:597
  27.9 24.5 %all_to_all.10.got_ref = bf16[8,2,96,384]{3,2,1,0:T(8,128)(2,1)S(1)} all-to-all(bf16[8,2,96,384]{3,2,1,0:T(8,128)(2,1)S(1)} %add_convert_fusion), channel_id=1, replica_groups={{0,32,64,96,128,160,192,224},{16,48,80,112,144,176,208,240},{1,33,65,97..., dimensions={0} | all-to-all | bytes 2359296 | tf_op jit(solution)/shard_map/all_to_all | solution.py:562
  52.4 0.4 deal.1
  52.7 30.2 %all_to_all.11.got_ref = bf16[16,16,384]{2,1,0:T(8,128)(2,1)S(1)} all-to-all(bf16[16,16,384]{2,1,0:T(8,128)(2,1)S(1)} %deal.1), channel_id=1, replica_groups=mesh['slide'=16,'rep'=16] {'rep'}, dimensions={0} | all-to-all | bytes 393216 | tf_op jit(solution)/shard_map/all_to_all | solution.py:599
  83.0 0.6 last.1
Async XLA Ops:
  1.3 5.1 %copy-start = (s32[1,1,16]{2,1,0:T(1,128)S(1)}, s32[1,1,16]{2,1,0:T(1,128)}, u32[]{:S(2)}) copy-start(s32[1,1,16]{2,1,0:T(1,128)} %param.23) | copy-start | bytes 196
  6.3 5.6 %collective-permute-start.2 = (bf16[7,14,32,384]{3,2,1,0:T(8,128)(2,1)}, bf16[7,14,32,384]{3,2,1,0:T(8,128)(2,1)S(1)}, u32[]{:S(2)}, u32[]{:S(2)}) collective-permute-start(bf16[7,14,32,384]{3,2,1,0:T(8,128)(2,1)} %get-tuple-element.7), channel_id=1, source_target_pairs={{0,16},{16,0},{32,48},{48,32},{64,80},{80,64},{96,112},{112,96},{1... | collective-permute-start | bytes 7225352 | tf_op jit(solution)/shard_map/ppermute | solution.py:590
  6.4 5.5 %collective-permute-start = (s32[16]{0:T(128)S(1)}, s32[16]{0:T(128)S(1)}, u32[]{:S(2)}, u32[]{:S(2)}) collective-permute-start(s32[16]{0:T(128)S(1)} %bitcast.8), channel_id=1, source_target_pairs={{0,16},{16,0},{32,48},{48,32},{64,80},{80,64},{96,112},{112,96},{1... | collective-permute-start | bytes 200 | tf_op jit(solution)/shard_map/ppermute | solution.py:585
  6.9 5.0 %collective-permute-start.1 = (s32[1]{0:T(128)}, s32[1]{0:T(128)}, u32[]{:S(2)}, u32[]{:S(2)}) collective-permute-start(s32[1]{0:T(128)} %bitcast.1), channel_id=1, source_target_pairs={{0,16},{16,0},{32,48},{48,32},{64,80},{80,64},{96,112},{112,96},{1... | collective-permute-start | bytes 20 | tf_op jit(solution)/shard_map/ppermute | solution.py:586
  11.9 0.5 copy-start.2
  11.9 1.4 %copy-start.1 = (bf16[7,14,32,384]{3,2,1,0:T(8,128)(2,1)}, bf16[7,14,32,384]{3,2,1,0:T(8,128)(2,1)S(1)}, u32[]{:S(2)}) copy-start(bf16[7,14,32,384]{3,2,1,0:T(8,128)(2,1)S(1)} %collective-permute-done.2.packed_hbm) | copy-start | bytes 7225348
  23.2 3.1 %collective-permute-start.3 = (bf16[8,2,96,384]{3,2,1,0:T(8,128)(2,1)}, bf16[8,2,96,384]{3,2,1,0:T(8,128)(2,1)S(1)}, u32[]{:S(2)}, u32[]{:S(2)}) collective-permute-start(bf16[8,2,96,384]{3,2,1,0:T(8,128)(2,1)} %get-tuple-element.9), channel_id=1, source_target_pairs={{0,16},{16,0},{32,48},{48,32},{64,80},{80,64},{96,112},{112,96},{1... | collective-permute-start | bytes 3538952 | tf_op jit(solution)/shard_map/ppermute | solution.py:596
where the time goes:
time: 83.6 us
  blocking collectives  54.7 us (65%)
  Pallas kernels  20.7 us (25%)
  waiting for transfers between devices  3.05 us (4%)
  other arithmetic  1.58 us (2%)
  local copies, waits for them, and re-layouts  1.43 us (2%)
  between operations  1.39 us (2%)
    all_to_all x1, blocking collectives, per_device(): return tuple(last(lax.all_to_all(got, 'rep', 0, 0, tiled=True)))  30.2 us
    all_to_all x1, blocking collectives, over_chips(): return lax.all_to_all(a, 'slide', 0, 0, tiled=True, axis_index_groups=cores)  24.5 us
    pallas_call x1, Pallas kernels, train(): pl.pallas_call(train_kernel, out_shape=[jax.ShapeDtypeStruct((PAIRS, 2, C...  9.87 us
    pallas_call x1, Pallas kernels, conv_first(): pl.pallas_call(first_kernel, out_shape=(jax.ShapeDtypeStruct(packed, jnp....  4.96 us
    pallas_call x1, Pallas kernels, conv_other(): pl.pallas_call(other_kernel, out_shape=jax.ShapeDtypeStruct((2, blocks *...  4.86 us
    ppermute x1, waiting for transfers between devices, per_device(): got = lax.ppermute(send, 'slide', swap)  3.05 us
  transfers between devices with their start and end apart: 4, of which 1 were waited for; matrix products, arithmetic and copies ran while one was open for 0% of the time, Pallas kernels for 6%

commit v1 on v0

--- a/solution.py
+++ b/solution.py
@@ -14,7 +14,7 @@
 KEPT = 9
 FIRST = 2
 ROWS = BAND_ROWS + 2 * MARGIN
-HID_STEP = 768
+HID_STEP = 1536
 SPAN = GROUP * BAND_TOK
 GROUPS = SLOTS // GROUP
 PAIRS = 8
@@ -95,10 +95,11 @@
     column = lax.broadcasted_iota(jnp.int32, (8, 128), 0)
     for lanes in range(0, channels, 128):
         part = slice(lanes, lanes + 128)
+        flat = image[:, :, part].astype(jnp.float32)
         for row in range(BAND_ROWS):
             sums = [None] * 7
             for dy in range(7):
-                x = image[row + dy, :, part].astype(jnp.float32)
+                x = flat[row + dy]
                 for dx in range(7):
                     term = x * taps[dy, dx : dx + 1, part]
                     sums[dx] = term if sums[dx] is None else sums[dx] + term
@@ -459,7 +460,7 @@
             pltpu.SemaphoreType.DMA((blocks, 4)),
             pltpu.SemaphoreType.DMA((blocks,)),
         ],
-        compiler_params=params(56),
+        compiler_params=params(62),
         cost_estimate=pl.CostEstimate(flops=8 * 10**9, bytes_accessed=10**7, transcendentals=0),
         name="conv_other",
     )(slots, count, tile_images, cotangent, *conv_weights, scale)

time: 83.6 us -> 79.4 us (0.950)
  blocking collectives: 54.7 us -> 52.5 us
  Pallas kernels: 20.7 us -> 19.3 us
  local copies, waits for them, and re-layouts: 1.43 us -> 0.51 us
    all_to_all x1, blocking collectives: 30.2 us -> 27.2 us  [per_device(): return tuple(last(lax.all_to_all(got, 'rep', 0, 0, tiled=True)))]
    pallas_call x1, Pallas kernels: 4.86 us -> 3.82 us  [conv_other(): pl.pallas_call(other_kernel, out_shape=jax.ShapeDtypeStruct((2, blocks *...]
    unnamed x6 -> x4, local copies, waits for them, and re-layouts: 1.43 us -> 0.51 us
    all_to_all x1, blocking collectives: 24.5 us -> 25.3 us  [over_chips(): return lax.all_to_all(a, 'slide', 0, 0, tiled=True, axis_index_groups=cores)]
  transfers between devices with their start and end apart: 4 -> 4, of which waited for: 1 -> 2; matrix products, arithmetic and copies ran while one was open for 0% -> 0% of each run, Pallas kernels for 6% -> 5%
where the time goes in v1:
time: 79.4 us; the launch traced here: 79.6 us
  blocking collectives  52.5 us (66%)
  Pallas kernels  19.3 us (24%)
  waiting for transfers between devices  3.55 us (4%)
  other arithmetic  1.58 us (2%)
  between operations  1.36 us (2%)
    all_to_all x1, blocking collectives, per_device(): return tuple(last(lax.all_to_all(got, 'rep', 0, 0, tiled=True)))  27.2 us
    all_to_all x1, blocking collectives, over_chips(): return lax.all_to_all(a, 'slide', 0, 0, tiled=True, axis_index_groups=cores)  25.3 us
    pallas_call x1, Pallas kernels, train(): pl.pallas_call(train_kernel, out_shape=[jax.ShapeDtypeStruct((PAIRS, 2, C...  9.61 us
    pallas_call x1, Pallas kernels, conv_first(): pl.pallas_call(first_kernel, out_shape=(jax.ShapeDtypeStruct(packed, jnp....  4.89 us
    pallas_call x1, Pallas kernels, conv_other(): pl.pallas_call(other_kernel, out_shape=jax.ShapeDtypeStruct((2, blocks *...  3.82 us
    ppermute x1, waiting for transfers between devices, per_device(): got = lax.ppermute(send, 'slide', swap)  3.05 us
  transfers between devices with their start and end apart: 4, of which 2 were waited for; matrix products, arithmetic and copies ran while one was open for 0% of the time, Pallas kernels for 5%

profile of v1, /device:TPU:2, one launch (start us, length us, event | category | flops | bytes accessed | tf_op | source)
XLA Modules:
  0.0 79.6 jit_solution(15739500273138588349)
XLA Ops:
  1.3 0.0 copy-start
  1.3 4.9 %conv_first.1 = (bf16[7,14,32,384]{3,2,1,0:T(8,128)(2,1)}, bf16[2,256,384]{2,1,0:T(8,128)(2,1)}) custom-call(s32[16]{0:T(128)} %bitcast.5, s32[1]{0:T(128)} %bitcast.3.refs_0_, bf16[4,32,32,384]{3,2,1,0:T(8,128)(2,1)} %refs_1_.3, bf16[4,32,32,384]{3,2,1,0:T(8,128)(2,1)} %refs_2_.3, bf16[7,7,384]{2,1,0:T(8,128)(2,1)} %taps_ref.1, f32[384]{0:T(512)} %depth_bias_ref.1, ...), custom_call_target="tpu_custom_call" | custom-call | tf_op jit(solution)/shard_map/conv_first/pallas_call | solution.py:427
  6.2 0.1 collective-permute-start.2
  6.3 0.0 copy-done
  6.3 0.5 collective-permute-start
  6.8 0.1 collective-permute-start.1
  6.9 3.8 %conv_other.1.other_hbm = bf16[2,896,384]{2,1,0:T(8,128)(2,1)} custom-call(s32[16]{0:T(128)} %bitcast.6, s32[1]{0:T(128)} %bitcast.4.refs_0_, bf16[4,32,32,384]{3,2,1,0:T(8,128)(2,1)} %refs_1_.3, bf16[4,32,32,384]{3,2,1,0:T(8,128)(2,1)} %refs_2_.3, bf16[7,7,384]{2,1,0:T(8,128)(2,1)} %taps_ref.1, f32[384]{0:T(512)} %depth_bias_ref.1, f32[384]{0:T(512)} %gain_ref.1, ...), custom_call_target="tpu_custom_call" | custom-call | flops 8000000000 | bytes 10000000 | tf_op jit(solution)/shard_map/conv_other/pallas_call | solution.py:452
  10.7 0.5 collective-permute-done.1.count_there_ref
  11.2 0.0 collective-permute-done.there_ref
  11.2 0.0 copy-start.1
  11.2 0.0 collective-permute-done.2.packed_hbm
  11.2 0.5 copy-done.1
  11.7 9.6 %train.1 = (bf16[8,2,96,384]{3,2,1,0:T(8,128)(2,1)}, bf16[8,2,96,384]{3,2,1,0:T(8,128)(2,1)}) custom-call(s32[16]{0:T(128)} %bitcast.7, s32[16]{0:T(128)} %copy-done.1, s32[1]{0:T(128)} %collective-permute-done.1.count_there_ref, s32[1]{0:T(128)} %bitcast.2.core_ref, bf16[2,256,384]{2,1,0:T(8,128)(2,1)} %get-tuple-element.6.first_hbm, ...), custom_call_target="tpu_custom_call" | custom-call | flops 8999999488 | bytes 10000000 | tf_op jit(solution)/shard_map/train/pallas_call | solution.py:475
  21.4 0.1 collective-permute-start.3
  21.5 3.0 %collective-permute-done.3 = bf16[8,2,96,384]{3,2,1,0:T(8,128)(2,1)S(1)} collective-permute-done((bf16[8,2,96,384]{3,2,1,0:T(8,128)(2,1)}, bf16[8,2,96,384]{3,2,1,0:T(8,128)(2,1)S(1)}, u32[]{:S(2)}, u32[]{:S(2)}) %collective-permute-start.3) | collective-permute-done | bytes 1179680 | tf_op jit(solution)/shard_map/ppermute | solution.py:597
  24.5 1.6 %add_convert_fusion = bf16[8,2,96,384]{3,2,1,0:T(8,128)(2,1)S(1)} fusion(bf16[8,2,96,384]{3,2,1,0:T(8,128)(2,1)S(1)} %collective-permute-done.3, bf16[8,2,96,384]{3,2,1,0:T(8,128)(2,1)} %get-tuple-element.8), kind=kLoop, calls=%fused_computation | loop fusion | flops 2359296 | bytes 3538944 | tf_op jit(solution)/shard_map/convert_element_type | solution.py:598
  26.1 25.3 %all_to_all.10.got_ref = bf16[8,2,96,384]{3,2,1,0:T(8,128)(2,1)S(1)} all-to-all(bf16[8,2,96,384]{3,2,1,0:T(8,128)(2,1)S(1)} %add_convert_fusion), channel_id=1, replica_groups={{0,32,64,96,128,160,192,224},{16,48,80,112,144,176,208,240},{1,33,65,97..., dimensions={0} | all-to-all | bytes 2359296 | tf_op jit(solution)/shard_map/all_to_all | solution.py:563
  51.4 0.4 deal.1
  51.8 27.2 %all_to_all.11.got_ref = bf16[16,16,384]{2,1,0:T(8,128)(2,1)S(1)} all-to-all(bf16[16,16,384]{2,1,0:T(8,128)(2,1)S(1)} %deal.1), channel_id=1, replica_groups=mesh['slide'=16,'rep'=16] {'rep'}, dimensions={0} | all-to-all | bytes 393216 | tf_op jit(solution)/shard_map/all_to_all | solution.py:600
  79.0 0.6 last.1
Async XLA Ops:
  1.3 5.0 %copy-start = (s32[1,1,16]{2,1,0:T(1,128)S(1)}, s32[1,1,16]{2,1,0:T(1,128)}, u32[]{:S(2)}) copy-start(s32[1,1,16]{2,1,0:T(1,128)} %param.23) | copy-start | bytes 196
  6.2 5.0 %collective-permute-start.2 = (bf16[7,14,32,384]{3,2,1,0:T(8,128)(2,1)}, bf16[7,14,32,384]{3,2,1,0:T(8,128)(2,1)}, u32[]{:S(2)}, u32[]{:S(2)}) collective-permute-start(bf16[7,14,32,384]{3,2,1,0:T(8,128)(2,1)} %get-tuple-element.7), channel_id=1, source_target_pairs={{0,16},{16,0},{32,48},{48,32},{64,80},{80,64},{96,112},{112,96},{1... | collective-permute-start | bytes 7225352 | tf_op jit(solution)/shard_map/ppermute | solution.py:591
  6.3 4.9 %collective-permute-start = (s32[16]{0:T(128)S(1)}, s32[16]{0:T(128)S(1)}, u32[]{:S(2)}, u32[]{:S(2)}) collective-permute-start(s32[16]{0:T(128)S(1)} %bitcast.8), channel_id=1, source_target_pairs={{0,16},{16,0},{32,48},{48,32},{64,80},{80,64},{96,112},{112,96},{1... | collective-permute-start | bytes 200 | tf_op jit(solution)/shard_map/ppermute | solution.py:586
  6.8 4.4 %collective-permute-start.1 = (s32[1]{0:T(128)}, s32[1]{0:T(128)}, u32[]{:S(2)}, u32[]{:S(2)}) collective-permute-start(s32[1]{0:T(128)} %bitcast.1), channel_id=1, source_target_pairs={{0,16},{16,0},{32,48},{48,32},{64,80},{80,64},{96,112},{112,96},{1... | collective-permute-start | bytes 20 | tf_op jit(solution)/shard_map/ppermute | solution.py:587
  11.2 0.5 copy-start.1
  21.4 3.1 %collective-permute-start.3 = (bf16[8,2,96,384]{3,2,1,0:T(8,128)(2,1)}, bf16[8,2,96,384]{3,2,1,0:T(8,128)(2,1)S(1)}, u32[]{:S(2)}, u32[]{:S(2)}) collective-permute-start(bf16[8,2,96,384]{3,2,1,0:T(8,128)(2,1)} %get-tuple-element.9), channel_id=1, source_target_pairs={{0,16},{16,0},{32,48},{48,32},{64,80},{80,64},{96,112},{112,96},{1... | collective-permute-start | bytes 3538952 | tf_op jit(solution)/shard_map/ppermute | solution.py:597
